TPU v7x, 256 devices: a whole 4x4x8 slice. The times are simulated.
256 devices in a mesh: cgrp: 8 (over z), dev: 32 (over x, y, core).
Axes of the slice: x: 4, y: 4, z: 8, core: 2. Of those that a mesh axis runs over, the one named last changes fastest.
Arguments:
- docs: bfloat16 [65536, 1024], P('dev'), may hold values from -140 to 140
- centroids: float32 [8192, 1024], P(('cgrp', 'dev')), may hold values from -6 to 6
Outputs:
- centroids_next: float32 [8192, 1024], P(('cgrp', 'dev'))
- mass: float32 [8192], P(('cgrp', 'dev'))
- doc_lse: float32 [65536], P('dev')
All inputs are finite; a program needn't handle non-finite values.
Results may differ from a plain program's by a relative error of at most 0.012.
The roundings to bfloat16 on the way count: a program that leaves them out, or rounds other values in their place, can miss the bound.
Values may be sent and summed in bfloat16 or wider, within the bound.
A program may use at most 64 MiB of HBM per device.

v0:
```python
import math

import jax
import jax.numpy as jnp
from jax import lax
from jax.sharding import PartitionSpec as P


def body(docs, centroids):
    width = docs.shape[1]
    scale = 4.0 / math.sqrt(width)
    rounded = centroids.astype(jnp.bfloat16)
    gathered = lax.all_gather(rounded, "dev", axis=0, tiled=True)
    gathered_wide = gathered.astype(jnp.float32)
    gathered_norms = jnp.sum(gathered_wide * gathered_wide, axis=1)
    dots = lax.dot_general(
        docs, gathered, (((1,), (1,)), ((), ())), preferred_element_type=jnp.float32
    )
    scores = (dots - 0.5 * gathered_norms[None, :]) * scale
    local_max = jnp.max(scores, axis=1)
    local_sum = jnp.sum(jnp.exp(scores - local_max[:, None]), axis=1)
    group_top = lax.pmax(local_max, "cgrp")
    group_sum = lax.psum(local_sum * jnp.exp(local_max - group_top), "cgrp")
    doc_lse = group_top + jnp.log(group_sum)
    resp = jnp.exp(scores - doc_lse[:, None])
    docs_wide = docs.astype(jnp.float32)
    local_mass = jnp.sum(resp, axis=0)
    term = lax.dot_general(
        resp,
        docs_wide,
        (((0,), (0,)), ((), ())),
        preferred_element_type=jnp.float32,
        precision=lax.Precision.HIGHEST,
    )
    weighted, mass = (
        lax.psum_scatter(term, "dev", scatter_dimension=0, tiled=True),
        lax.psum_scatter(local_mass, "dev", scatter_dimension=0, tiled=True),
    )
    centroids_next = (weighted + centroids) / (mass[:, None] + 1.0)
    return (centroids_next, mass, doc_lse)


def solution(mesh):
    in_specs = (P("dev", None), P(("cgrp", "dev"), None))
    out_specs = (P(("cgrp", "dev"), None), P(("cgrp", "dev")), P("dev"))
    return jax.shard_map(body, mesh=mesh, in_specs=in_specs, out_specs=out_specs, check_vma=False)
```

profile of v0, /device:TPU:1, one launch (start us, length us, event | category | flops | bytes accessed | tf_op | source)
XLA Modules:
  0.0 227.0 jit_solution(16202654459003388817)
XLA Ops:
  7.2 0.0 all-gather.2.cloned.1.call-start
  7.2 1.5 convert_element_type.7
  8.8 0.0 all-gather.2.cloned.1.call-update
  8.8 0.0 reduce-scatter.2.cloned.1.call-start
  8.8 55.4 %all-gather.2.cloned.1.call-done = bf16[1024,1024]{1,0:T(8,128)(2,1)} async-done(((bf16[32,1024]{1,0:T(8,128)(2,1)}), bf16[1024,1024]{1,0:T(8,128)(2,1)}) %all-gather.2.cloned.1.call-update) | async-done | bytes 2097168 | tf_op jit(solution)/shard_map/all_gather | solution.py:13
  64.2 2.1 multiply_reduce_fusion
  66.3 10.6 %fusion.2 = (f32[2048]{0:T(1024)S(1)}, f32[2048,1024]{0,1:T(8,128)}) fusion(f32[1024]{0:T(1024)S(1)} %broadcast_multiply_fusion, bf16[2048,1024]{1,0:T(8,128)(2,1)} %param.2, bf16[1024,1024]{1,0:T(8,128)(2,1)} %all-gather.2.cloned.1.call-done), kind=kOutput, calls=%fused_computation.5 | convolution fusion | flops 4301256704 | bytes 14692352 | tf_op jit(solution)/shard_map/dot_general | solution.py:16
  76.9 14.0 %pmax.7 = f32[2048]{0:T(1024)S(1)} all-reduce(f32[2048]{0:T(1024)S(1)} %get-tuple-element.5), channel_id=1, replica_groups=mesh['cgrp'=8,'dev'=32] {'cgrp'}, use_global_device_ids=true, to_apply=%region_2.0 | all-reduce | flops 2048 | bytes 16384 | tf_op jit(solution)/shard_map/pmax | solution.py:22
  91.0 4.5 %exponential_reduce_fusion = f32[2048]{0:T(1024)S(1)} fusion(f32[2048,1024]{0,1:T(8,128)} %get-tuple-element.6, f32[2048]{0:T(1024)S(1)} %get-tuple-element.5, f32[1024]{0:T(1024)S(1)} %broadcast_multiply_fusion), kind=kLoop, calls=%fused_computation.1 | loop fusion | flops 8386560 | bytes 8409088 | tf_op jit(solution)/shard_map/reduce_sum | solution.py:21
  95.5 11.6 %psum.7 = f32[2048]{0:T(1024)S(1)} all-reduce(f32[2048]{0:T(1024)S(1)} %exponential_multiply_fusion), channel_id=1, replica_groups=mesh['cgrp'=8,'dev'=32] {'cgrp'}, use_global_device_ids=true, to_apply=%region_4.0 | all-reduce | flops 2048 | bytes 16384 | tf_op jit(solution)/shard_map/psum | solution.py:23
  107.1 0.0 copy-start.1
  107.1 0.0 copy-start.2
  107.2 19.1 %fusion.1 = f32[1024,1024]{1,0:T(8,128)} fusion(bf16[2048,1024]{1,0:T(8,128)(2,1)} %param.2, f32[2048,1024]{0,1:T(8,128)} %get-tuple-element.6, f32[2048]{0:T(1024)S(1)} %log_add_fusion, f32[1024]{0:T(1024)S(1)} %broadcast_multiply_fusion), kind=kOutput, calls=%fused_computation.4 | convolution fusion | flops 25776095232 | bytes 16789504 | tf_op jit(solution)/shard_map/dot_general | solution.py:28
  126.3 0.0 copy-start
  126.3 0.0 reduce-scatter.2.cloned.1.call-update
  126.3 0.0 copy-done.2
  126.3 0.6 dynamic-slice
  127.5 0.0 copy-done.1
  127.6 4.5 %fusion = f32[1024]{0:T(1024)S(1)} fusion(f32[2048,1024]{0,1:T(8,128)} %get-tuple-element.6, f32[2048]{0:T(1024)S(1)} %log_add_fusion, f32[1024]{0:T(1024)S(1)} %broadcast_multiply_fusion), kind=kLoop, calls=%fused_computation.3 | loop fusion | flops 8387584 | bytes 8404992 | tf_op jit(solution)/shard_map/reduce_sum | solution.py:27
  132.1 69.9 %all-reduce = f32[1024]{0:T(1024)S(1)} all-reduce(f32[1024]{0:T(1024)S(1)} %fusion), channel_id=3, replica_groups=mesh['cgrp'=8,'dev'=32] {'dev'}, use_global_device_ids=true, to_apply=%region_7.0.clone | all-reduce | flops 1024 | bytes 8192
  202.0 0.6 broadcast_add_fusion
  202.5 16.0 %reduce-scatter.2.cloned.1.call-done = f32[32,1024]{1,0:T(8,128)} async-done(((f32[1024,1024]{1,0:T(8,128)}), f32[32,1024]{1,0:T(8,128)}) %reduce-scatter.2.cloned.1.call-update) | async-done | bytes 131088 | tf_op jit(solution)/shard_map/reduce_scatter | solution.py:36
  218.6 0.0 copy-done
  218.6 1.6 add_divide_fusion
  (3 shorter events, 0.0 us)
Async XLA Ops:
  7.2 57.1 %all-gather.2.cloned.1.call-start = ((), (), s32[]{:S(2)}) async-start(), calls=%async_computation.1 | async-start | bytes 2162688 | tf_op jit(solution)/shard_map/all_gather | solution.py:13
  8.8 209.8 %reduce-scatter.2.cloned.1.call-start = ((), (), s32[]{:S(2)}) async-start(), calls=%async_computation.2 | async-start | bytes 4325376 | tf_op jit(solution)/shard_map/reduce_scatter | solution.py:36
  107.1 20.4 %copy-start.1 = (f32[2048]{0:T(1024)}, f32[2048]{0:T(1024)S(1)}, u32[]{:S(2)}) copy-start(f32[2048]{0:T(1024)S(1)} %log_add_fusion) | copy-start | bytes 24580
  107.1 19.2 %copy-start.2 = (u32[256]{0:T(256)S(1)}, u32[256]{0:T(256)}, u32[]{:S(2)}) copy-start(u32[256]{0:T(256)} %constant.13) | copy-start | bytes 3076
  126.3 92.3 %copy-start = (f32[32,1024]{1,0:T(8,128)S(1)}, f32[32,1024]{1,0:T(8,128)}, u32[]{:S(2)}) copy-start(f32[32,1024]{1,0:T(8,128)} %param.3) | copy-start | bytes 393220
Sparse Core Ops, SparseCore 0:
  11.1 53.0 all-gather.1
  126.4 92.0 reduce-scatter.1
where the time goes:
time: 228 us; the launch traced here: 227 us
  blocking collectives  95.5 us (42%)
  waiting for transfers between devices  71.5 us (31%)
  matrix products  29.7 us (13%)
  other arithmetic  14.9 us (7%)
  between operations  14.8 us (6%)
    unnamed x1, blocking collectives  69.9 us
    all_gather x1, waiting for transfers between devices, body(): gathered = lax.all_gather(rounded, 'dev', axis=0, tiled=True)  55.4 us
    dot_general x1, matrix products, body(): lax.dot_general(resp, docs_wide, (((0,), (0,)), ((), ())), preferred_elem...  19.1 us
    reduce_scatter x1, waiting for transfers between devices, body(): lax.psum_scatter(term, 'dev', scatter_dimension=0, tiled=True)  16 us
    pmax x1, blocking collectives, body(): group_top = lax.pmax(local_max, 'cgrp')  14 us
    psum x1, blocking collectives, body(): group_sum = lax.psum(local_sum * jnp.exp(local_max - group_top), 'cgrp')  11.6 us
    dot_general x1, matrix products, body(): lax.dot_general(docs, gathered, (((1,), (1,)), ((), ())), preferred_eleme...  10.6 us
  transfers between devices with their start and end apart: 2, of which 2 were waited for; matrix products, arithmetic and copies ran while one was open for 3% of the time, Pallas kernels for 0%

commit v1 on v0

v1 whole, which is shorter than its diff:
```python
import jax
import jax.numpy as jnp
from jax import lax
from jax.experimental import pallas as pl
from jax.experimental.pallas import tpu as pltpu
from jax.sharding import PartitionSpec as P

MESH = pl.DeviceIdType.MESH
WIDTH = 1024
DOCS = 2048
ROWS = 32
HALF = 128
WIDE = WIDTH + 128
SCALE = 0.125
TILE = 256


def em_kernel(
    docs_hbm, cent_ref, acc_ref, lse_ref,
    docs, mine, sib, expo, top, total, lses, factor,
    keep, out_sib, in_sib, out_v, in_v, out_a, in_a,
    docs_sem, s1, r1, s2, r2, s3, r3, s4, r4, s5, r5, s6, r6, s7, r7,
):
    z = lax.axis_index("cgrp")
    dev = lax.axis_index("dev")
    core = lax.rem(dev, 2)
    x = lax.div(dev, 8)
    y = lax.rem(lax.div(dev, 2), 4)
    a = x * (1 - core) + y * core
    v = y * (1 - core) + x * core

    def rot(p, k):
        return lax.rem(p + (k + 4), 4)

    def at(ai, vi):
        xi = ai * (1 - core) + vi * core
        yi = vi * (1 - core) + ai * core
        return (z, (xi * 4 + yi) * 2 + core)

    sibling = (z, dev + 1 - 2 * core)

    def up(k):
        return (lax.rem(z + k, 8), dev)

    def rows(i):
        return pl.ds(pl.multiple_of(i * ROWS, ROWS), ROWS)

    def remote(src, dst, send, recv, where):
        return pltpu.make_async_remote_copy(
            src_ref=src, dst_ref=dst, send_sem=send, recv_sem=recv, device_id=where, device_id_type=MESH
        )

    load = pltpu.make_async_copy(docs_hbm, docs, docs_sem)
    load.start()
    barrier = pltpu.get_barrier_semaphore()
    greet = [at(a, rot(v, k)) for k in (1, 2, 3)] + [at(rot(a, k), v) for k in (1, 2, 3)]
    greet += [sibling] + [up(k) for k in range(1, 8)]
    for where in greet:
        pl.semaphore_signal(barrier, inc=1, device_id=where, device_id_type=MESH)
    mine[a, rows(v)] = cent_ref[...].astype(jnp.bfloat16)
    pl.semaphore_wait(barrier, len(greet))

    def block(da, dj):
        return mine.at[rot(a, -da), rows(rot(v, -dj))]

    def along_v(dv):
        return remote(block(0, 0), block(0, 0), s1.at[dv], r1.at[dv], at(a, rot(v, dv)))

    def arrived_v(dv):
        return remote(block(0, dv), block(0, dv), s1.at[dv], r1.at[dv], at(a, rot(v, dv)))

    def along_a(da, dj):
        return remote(block(0, dj), block(0, dj), s2.at[da, dj], r2.at[da, dj], at(rot(a, da), v))

    def arrived_a(da, dj):
        return remote(block(da, dj), block(da, dj), s2.at[da, dj], r2.at[da, dj], at(rot(a, da), v))

    def across(da, dj):
        where = sib.at[rot(a, -da), rows(rot(v, -dj))]
        return remote(block(da, dj), where, s3.at[da, dj], r3.at[da, dj], sibling)

    def arrived_across(da, dj):
        where = sib.at[rot(v, -da), rows(rot(a, -dj))]
        return remote(where, where, s3.at[da, dj], r3.at[da, dj], sibling)

    def scores(t):
        for dj in (0, 1, 3, 2):
            arrived_across(t, dj).wait_recv()
        cent = jnp.concatenate([mine[rot(a, -t)], sib[rot(v, -t)]], axis=0)
        wide = cent.astype(jnp.float32)
        bias = jnp.sum(wide * wide, axis=1, keepdims=True) * (0.5 * SCALE)
        for i in range(DOCS // TILE):
            part = pl.ds(i * TILE, TILE)
            dots = lax.dot_general(
                cent, docs[part, :], (((1,), (1,)), ((), ())), preferred_element_type=jnp.float32
            )
            s = dots * SCALE - bias
            m = jnp.max(s, axis=0, keepdims=True)
            p = jnp.exp(s - m)
            expo[t, :, part] = p.astype(jnp.bfloat16)
            top[t, :, part] = m
            total[t, :, part] = jnp.sum(p, axis=0, keepdims=True)

    for dv in (1, 3, 2):
        along_v(dv).start()
    for da in (1, 3, 2):
        along_a(da, 0).start()
    across(0, 0).start()
    for dv in (1, 3, 2):
        arrived_v(dv).wait_recv()
        for da in (1, 3, 2):
            along_a(da, dv).start()
        across(0, dv).start()
    load.wait()
    scores(0)
    for da in (1, 3):
        for dj in (0, 1, 3, 2):
            arrived_a(da, dj).wait_recv()
            across(da, dj).start()
    scores(1)
    for dj in (0, 1):
        arrived_a(2, dj).wait_recv()
        across(2, dj).start()
    scores(3)
    for dj in (3, 2):
        arrived_a(2, dj).wait_recv()
        across(2, dj).start()
    scores(2)

    m = jnp.maximum(jnp.maximum(top[0], top[1]), jnp.maximum(top[2], top[3]))
    l = sum(total[t] * jnp.exp(top[t] - m) for t in range(4))
    lses[z] = m + jnp.log(l)

    def along_z(k):
        return remote(lses.at[z], lses.at[z], s4.at[k], r4.at[k], up(k))

    def arrived_z(k):
        where = lses.at[lax.rem(z + 8 - k, 8)]
        return remote(where, where, s4.at[k], r4.at[k], up(k))

    for k in (4, 3, 5, 2, 6, 1, 7):
        along_z(k).start()
    for k in (1, 7, 2, 6, 3, 5, 4):
        arrived_z(k).wait_recv()
    m = lses[0]
    for k in range(1, 8):
        m = jnp.maximum(m, lses[k])
    lse = m + jnp.log(sum(jnp.exp(lses[k] - m) for k in range(8)))
    lse_ref[...] = lse
    for t in range(4):
        factor[t] = jnp.exp(top[t] - lse)

    def give(t):
        return remote(out_sib.at[t], in_sib.at[t], s5.at[t], r5.at[t], sibling)

    def sum_v(t, dv):
        return remote(
            out_v.at[t, rows(rot(v, dv))], in_v.at[t, dv - 1], s6.at[t, dv], r6.at[t, dv], at(a, rot(v, dv))
        )

    def sum_a(t):
        return remote(out_a.at[t - 1], in_a.at[t - 1], s7.at[t], r7.at[t], at(rot(a, -t), v))

    def weigh(t):
        resp = expo[t].astype(jnp.float32) * factor[t]
        mass = jnp.broadcast_to(jnp.sum(resp, axis=1, keepdims=True), (2 * HALF, 128))
        keep[t, :, pl.ds(WIDTH, 128)] = mass[:HALF]
        out_sib[t, :, pl.ds(WIDTH, 128)] = mass[HALF:].astype(jnp.bfloat16)
        resp = resp.astype(jnp.bfloat16)
        for j in range(WIDTH // TILE):
            part = pl.ds(j * TILE, TILE)
            term = jnp.dot(resp, docs[:, part], preferred_element_type=jnp.float32)
            keep[t, :, part] = term[:HALF]
            out_sib[t, :, part] = term[HALF:].astype(jnp.bfloat16)
        give(t).start()

    def pair(t):
        give(t).wait_recv()
        both = keep[t] + in_sib[t].astype(jnp.float32)
        keep[t] = both
        out_v[t] = both.astype(jnp.bfloat16)
        for dv in (2, 1, 3):
            sum_v(t, dv).start()

    def row(t):
        for dv in (1, 3, 2):
            sum_v(t, dv).wait_recv()
        own = keep[t, rows(v)]
        for dv in (1, 2, 3):
            own = own + in_v[t, dv - 1].astype(jnp.float32)
        if t == 0:
            return own
        out_a[t - 1] = own.astype(jnp.bfloat16)
        sum_a(t).start()

    weigh(2)
    weigh(1)
    pair(2)
    weigh(3)
    pair(1)
    weigh(0)
    pair(3)
    pair(0)
    row(2)
    row(1)
    row(3)
    acc = row(0)
    for t in (1, 3, 2):
        sum_a(t).wait_recv()
        acc = acc + in_a[t - 1].astype(jnp.float32)
    acc_ref[...] = acc

    for dv in (1, 2, 3):
        along_v(dv).wait_send()
    for da in (1, 2, 3):
        for dj in range(4):
            along_a(da, dj).wait_send()
    for da in range(4):
        for dj in range(4):
            across(da, dj).wait_send()
    for k in range(1, 8):
        along_z(k).wait_send()
    for t in range(4):
        give(t).wait_send()
        for dv in (1, 2, 3):
            sum_v(t, dv).wait_send()
        if t:
            sum_a(t).wait_send()


def finish_kernel(acc_ref, lse_in, cent_ref, next_ref, mass_ref, lse_ref):
    mass = acc_ref[:, pl.ds(WIDTH, 128)]
    next_ref[...] = (acc_ref[:, pl.ds(0, WIDTH)] + cent_ref[...]) / (mass[:, :1] + 1.0)
    mass_ref[...] = jnp.transpose(mass)[0]
    lse_ref[...] = lse_in[0]


def body(docs, centroids):
    bf16, f32 = jnp.bfloat16, jnp.float32
    dma = pltpu.SemaphoreType.DMA
    vmem = pl.BlockSpec(memory_space=pltpu.VMEM)
    acc, lse = pl.pallas_call(
        em_kernel,
        out_shape=(jax.ShapeDtypeStruct((ROWS, WIDE), f32), jax.ShapeDtypeStruct((1, DOCS), f32)),
        in_specs=[pl.BlockSpec(memory_space=pl.ANY), vmem],
        out_specs=(vmem, vmem),
        scratch_shapes=[
            pltpu.VMEM((DOCS, WIDTH), bf16),
            pltpu.VMEM((4, HALF, WIDTH), bf16),
            pltpu.VMEM((4, HALF, WIDTH), bf16),
            pltpu.VMEM((4, 2 * HALF, DOCS), bf16),
            pltpu.VMEM((4, 1, DOCS), f32),
            pltpu.VMEM((4, 1, DOCS), f32),
            pltpu.VMEM((8, 1, DOCS), f32),
            pltpu.VMEM((4, 1, DOCS), f32),
            pltpu.VMEM((4, HALF, WIDE), f32),
            pltpu.VMEM((4, HALF, WIDE), bf16),
            pltpu.VMEM((4, HALF, WIDE), bf16),
            pltpu.VMEM((4, HALF, WIDE), bf16),
            pltpu.VMEM((4, 3, ROWS, WIDE), bf16),
            pltpu.VMEM((3, ROWS, WIDE), bf16),
            pltpu.VMEM((3, ROWS, WIDE), bf16),
            dma,
            dma((4,)), dma((4,)),
            dma((4, 4)), dma((4, 4)),
            dma((4, 4)), dma((4, 4)),
            dma((8,)), dma((8,)),
            dma((4,)), dma((4,)),
            dma((4, 4)), dma((4, 4)),
            dma((4,)), dma((4,)),
        ],
        compiler_params=pltpu.CompilerParams(
            collective_id=0, has_side_effects=True, vmem_limit_bytes=56 * 2**20
        ),
        cost_estimate=pl.CostEstimate(
            flops=4 * DOCS * WIDTH * 1024, bytes_accessed=2 * DOCS * WIDTH, transcendentals=DOCS * 1024
        ),
        name="em_step",
    )(docs, centroids)
    return pl.pallas_call(
        finish_kernel,
        out_shape=(
            jax.ShapeDtypeStruct((ROWS, WIDTH), f32),
            jax.ShapeDtypeStruct((ROWS,), f32),
            jax.ShapeDtypeStruct((DOCS,), f32),
        ),
        in_specs=[vmem] * 3,
        out_specs=(vmem,) * 3,
        name="finish",
    )(acc, lse, centroids)


def solution(mesh):
    in_specs = (P("dev", None), P(("cgrp", "dev"), None))
    out_specs = (P(("cgrp", "dev"), None), P(("cgrp", "dev")), P("dev"))
    return jax.shard_map(body, mesh=mesh, in_specs=in_specs, out_specs=out_specs, check_vma=False)
```

time: 228 us -> 51.3 us (0.22)
  blocking collectives: 95.5 us -> 0 us
  waiting for transfers between devices: 71.5 us -> 0 us
  Pallas kernels: 0 us -> 50.5 us
  matrix products: 29.7 us -> 0 us
  other arithmetic: 14.9 us -> 0 us
  between operations: 14.8 us -> 0.64 us
    unnamed x1 -> x0, blocking collectives: 69.9 us -> none
    all_gather x1 -> x0, waiting for transfers between devices: 55.4 us -> none  [body(): gathered = lax.all_gather(rounded, 'dev', axis=0, tiled=True)]
    pallas_call x0 -> x2, Pallas kernels: none -> 50.5 us  [the longest x1 48.8 us: body(): pl.pallas_call(em_kernel, out_shape=(jax.ShapeDtypeStruct((ROWS, WIDE), f...]
    dot_general x2 -> x0, matrix products: 29.7 us -> none  [the longest x1 19.1 us: body(): lax.dot_general(resp, docs_wide, (((0,), (0,)), ((), ())), preferred_elem...]
    reduce_scatter x1 -> x0, waiting for transfers between devices: 16 us -> none  [body(): lax.psum_scatter(term, 'dev', scatter_dimension=0, tiled=True)]
    pmax x1 -> x0, blocking collectives: 14 us -> none  [body(): group_top = lax.pmax(local_max, 'cgrp')]
    psum x1 -> x0, blocking collectives: 11.6 us -> none  [body(): group_sum = lax.psum(local_sum * jnp.exp(local_max - group_top), 'cgrp')]
    reduce_sum x3 -> x0, other arithmetic: 11.1 us -> none  [the longest x1 4.51 us: body(): local_sum = jnp.sum(jnp.exp(scores - local_max[:, None]), axis=1)]
  transfers between devices with their start and end apart: 2 -> 0, of which waited for: 2 -> 0; matrix products, arithmetic and copies ran while one was open for 3% -> 0% of each run, Pallas kernels for 0% -> 0%
where the time goes in v1:
time: 51.3 us; the launch traced here: 51.2 us
  Pallas kernels  50.5 us (98%)
  between operations  0.64 us (1%)
    pallas_call x1, Pallas kernels, body(): pl.pallas_call(em_kernel, out_shape=(jax.ShapeDtypeStruct((ROWS, WIDE), f...  48.8 us
    pallas_call x1, Pallas kernels, body(): pl.pallas_call(finish_kernel, out_shape=(jax.ShapeDtypeStruct((ROWS, WIDT...  1.74 us

profile of v1, /device:TPU:1, one launch (start us, length us, event | category | flops | bytes accessed | tf_op | source)
XLA Modules:
  0.0 51.2 jit_solution(16816022986587130123)
XLA Ops:
  0.6 48.8 %em_step.1 = (f32[32,1152]{1,0:T(8,128)}, f32[1,2048]{1,0:T(1,128)}) custom-call(bf16[2048,1024]{1,0:T(8,128)(2,1)} %docs_hbm.1, f32[32,1024]{1,0:T(8,128)} %cent_ref.3), custom_call_target="tpu_custom_call" | custom-call | flops 8589934592 | bytes 4194304 | tf_op jit(solution)/shard_map/em_step/pallas_call | solution.py:242
  49.4 1.7 %finish.1 = (f32[32,1024]{1,0:T(8,128)}, f32[32]{0:T(128)}, f32[2048]{0:T(1024)}) custom-call(f32[32,1152]{1,0:T(8,128)} %get-tuple-element.5.acc_ref, f32[1,2048]{1,0:T(1,128)} %get-tuple-element.6.lse_in, f32[32,1024]{1,0:T(8,128)} %cent_ref.3), custom_call_target="tpu_custom_call" | custom-call | tf_op jit(solution)/shard_map/finish/pallas_call | solution.py:280

commit v2 on v1

v2 whole, which is shorter than its diff:
```python
import jax
import jax.numpy as jnp
from jax import lax
from jax.experimental import pallas as pl
from jax.experimental.pallas import tpu as pltpu
from jax.sharding import PartitionSpec as P

MESH = pl.DeviceIdType.MESH
WIDTH = 1024
DOCS = 2048
ROWS = 32
HALF = 128
WIDE = WIDTH + 128
SCALE = 0.125
TILE = 256
GROUPS = 10


def em_kernel(
    docs_hbm, cent_hbm, acc_ref, lse_ref,
    docs, turned, cent, mine, sib, expo, top, total, lses, factor,
    keep, out_sib, in_sib, out_v, in_v, out_a, in_a,
    docs_sem, cent_sem, low_sem, high_sem,
    s1, r1, s2, r2, s3, r3, s4, r4, s5, r5, s6, r6, s7, r7,
):
    z = lax.axis_index("cgrp")
    dev = lax.axis_index("dev")
    core = lax.rem(dev, 2)
    x = lax.div(dev, 8)
    y = lax.rem(lax.div(dev, 2), 4)
    a = x * (1 - core) + y * core
    v = y * (1 - core) + x * core

    def at(da, dv):
        ai = lax.rem(a + (da + 4), 4)
        vi = lax.rem(v + (dv + 4), 4)
        xi = ai * (1 - core) + vi * core
        yi = vi * (1 - core) + ai * core
        return (z, (xi * 4 + yi) * 2 + core)

    sibling = (z, dev + 1 - 2 * core)

    def up(k):
        return (lax.rem(z + k, 8), dev)

    def rows(i, n=1):
        return pl.ds(i * ROWS, n * ROWS)

    def remote(src, dst, send, recv, where):
        return pltpu.make_async_remote_copy(
            src_ref=src, dst_ref=dst, send_sem=send, recv_sem=recv, device_id=where, device_id_type=MESH
        )

    def signal(sem, where):
        pl.semaphore_signal(sem, inc=1, device_id=where, device_id_type=MESH)

    barrier = pltpu.get_barrier_semaphore()
    greet = [at(0, 2), at(2, 0), at(0, 1), at(0, 3), at(1, 0), at(3, 0), sibling, up(1), up(7)]
    own = pltpu.make_async_copy(cent_hbm, cent, cent_sem)
    own.start()
    for where in greet:
        signal(barrier, where)
    load = pltpu.make_async_copy(docs_hbm, docs, docs_sem)
    load.start()
    own.wait()
    mine[0, rows(0)] = cent[...].astype(jnp.bfloat16)
    pl.semaphore_wait(barrier, len(greet))

    def tell_low():
        signal(low_sem, up(1))

    def tell_high():
        signal(high_sem, up(7))

    def told():
        pl.semaphore_wait(low_sem, 1)
        pl.semaphore_wait(high_sem, 1)

    def along_v(dv):
        return remote(mine.at[0, rows(0)], mine.at[0, rows(dv)], s1.at[dv], r1.at[dv], at(0, dv))

    def along_a(da, dj):
        return remote(mine.at[0, rows(dj)], mine.at[da, rows(dj)], s2.at[da, dj], r2.at[da, dj], at(da, 0))

    def across(da, dj):
        return remote(mine.at[da, rows(dj)], sib.at[da, rows(dj)], s3.at[da, dj], r3.at[da, dj], sibling)

    def scores(g, blocks):
        c = jnp.concatenate([b[t, rows(j, n)] for b, t, j, n, _ in blocks], axis=0)
        wide = c.astype(jnp.float32)
        bias = jnp.sum(wide * wide, axis=1, keepdims=True) * (0.5 * SCALE)
        for i in range(DOCS // TILE):
            part = pl.ds(i * TILE, TILE)
            dots = jnp.dot(c, turned[:, part], preferred_element_type=jnp.float32)
            s = dots * SCALE - bias
            m = jnp.max(s, axis=0, keepdims=True)
            p = jnp.exp(s - m)
            e = p.astype(jnp.bfloat16)
            done = 0
            for _, t, _, n, r in blocks:
                expo[t, rows(r, n), part] = e[done * ROWS:(done + n) * ROWS]
                done += n
            top[pl.ds(g, 1), part] = m
            total[pl.ds(g, 1), part] = jnp.sum(p, axis=0, keepdims=True)

    def from_mine(dj):
        return [(mine, da, dj, 1, dj) for da in (1, 2, 3)]

    def from_sib(dj):
        return [(sib, da, dj, 1, dj + 4) for da in (1, 2, 3)]

    def forward_a(dj):
        for da in (1, 3, 2):
            along_a(da, dj).wait_recv()
            across(da, dj).start()

    def wait_across(dj):
        for da in (1, 3, 2):
            across(da, dj).wait_recv()

    for dv in (1, 3, 2):
        along_v(dv).start()
    for da in (1, 3, 2):
        along_a(da, 0).start()
    across(0, 0).start()
    tell_low()
    tell_high()
    load.wait()
    for i in range(DOCS // TILE):
        part = pl.ds(i * TILE, TILE)
        turned[:, part] = jnp.transpose(docs[part, :])
    for dv in (1, 3, 2):
        along_v(dv).wait_recv()
        for da in (1, 3, 2):
            along_a(da, dv).start()
        across(0, dv).start()
    forward_a(0)
    told()
    tell_low()
    tell_high()
    scores(0, [(mine, 0, 0, 4, 0)])
    scores(1, from_mine(0))
    for dj in (0, 1, 3, 2):
        across(0, dj).wait_recv()
    scores(2, [(sib, 0, 0, 4, 4)])
    told()
    tell_low()
    wait_across(0)
    scores(3, from_sib(0))
    forward_a(1)
    scores(4, from_mine(1))
    forward_a(3)
    wait_across(1)
    scores(5, from_sib(1))
    scores(6, from_mine(3))
    forward_a(2)
    wait_across(3)
    scores(7, from_sib(3))
    scores(8, from_mine(2))
    wait_across(2)
    scores(9, from_sib(2))

    tops = top[...]
    m = jnp.max(tops, axis=0, keepdims=True)
    l = jnp.sum(total[...] * jnp.exp(tops - m), axis=0, keepdims=True)
    lses[z] = m + jnp.log(l)

    def along_z(k):
        return remote(lses.at[z], lses.at[z], s4.at[k], r4.at[k], up(k))

    def arrived_z(k):
        where = lses.at[lax.rem(z + 8 - k, 8)]
        return remote(where, where, s4.at[k], r4.at[k], up(k))

    pl.semaphore_wait(low_sem, 1)
    for k in (4, 3, 5, 2, 6, 1, 7):
        along_z(k).start()
    for k in (1, 7, 2, 6, 3, 5, 4):
        arrived_z(k).wait_recv()
    m = lses[0]
    for k in range(1, 8):
        m = jnp.maximum(m, lses[k])
    lse = m + jnp.log(sum(jnp.exp(lses[k] - m) for k in range(8)))
    lse_ref[...] = lse
    factor[...] = jnp.exp(tops - lse)

    def give(t):
        return remote(out_sib.at[t], in_sib.at[t], s5.at[t], r5.at[t], sibling)

    def sum_v(t, dv):
        return remote(
            out_v.at[t, rows(4 - dv)], in_v.at[t, dv - 1], s6.at[t, dv], r6.at[t, dv], at(0, dv)
        )

    def sum_a(t):
        return remote(out_a.at[t - 1], in_a.at[t - 1], s7.at[t], r7.at[t], at(-t, 0))

    def weigh(t, other, out):
        parts = [
            expo[t, rows(4 * other + dj)].astype(jnp.float32) * factor[pl.ds(first + step * other, 1), :]
            for dj, (first, step) in enumerate([(0, 2)] * 4 if t == 0 else [(1, 2), (4, 1), (8, 1), (6, 1)])
        ]
        resp = jnp.concatenate(parts, axis=0)
        mass = jnp.broadcast_to(jnp.sum(resp, axis=1, keepdims=True), (HALF, 128))
        out[t, :, pl.ds(WIDTH, 128)] = mass.astype(out.dtype)
        resp = resp.astype(jnp.bfloat16)
        for j in range(WIDTH // TILE):
            part = pl.ds(j * TILE, TILE)
            term = jnp.dot(resp, docs[:, part], preferred_element_type=jnp.float32)
            out[t, :, part] = term.astype(out.dtype)

    def theirs(t):
        weigh(t, 1, out_sib)
        give(t).start()

    def ours(t):
        weigh(t, 0, keep)

    def pair(t):
        give(t).wait_recv()
        both = keep[t] + in_sib[t].astype(jnp.float32)
        keep[t] = both
        out_v[t] = both.astype(jnp.bfloat16)
        for dv in (2, 1, 3):
            sum_v(t, dv).start()

    def row(t):
        for dv in (1, 3, 2):
            sum_v(t, dv).wait_recv()
        own = keep[t, rows(0)]
        for dv in (1, 2, 3):
            own = own + in_v[t, dv - 1].astype(jnp.float32)
        if t == 0:
            return own
        out_a[t - 1] = own.astype(jnp.bfloat16)
        sum_a(t).start()

    theirs(2)
    ours(2)
    theirs(1)
    pair(2)
    ours(1)
    theirs(3)
    pair(1)
    ours(3)
    theirs(0)
    pair(3)
    ours(0)
    pair(0)
    row(2)
    row(1)
    row(3)
    acc = row(0)
    for t in (1, 3, 2):
        sum_a(t).wait_recv()
        acc = acc + in_a[t - 1].astype(jnp.float32)
    acc_ref[...] = acc

    for dv in (1, 2, 3):
        along_v(dv).wait_send()
    for da in (1, 2, 3):
        for dj in range(4):
            along_a(da, dj).wait_send()
    for da in range(4):
        for dj in range(4):
            across(da, dj).wait_send()
    for k in range(1, 8):
        along_z(k).wait_send()
    for t in range(4):
        give(t).wait_send()
        for dv in (1, 2, 3):
            sum_v(t, dv).wait_send()
        if t:
            sum_a(t).wait_send()


def finish_kernel(acc_ref, lse_in, cent_ref, next_ref, mass_ref, lse_ref):
    mass = acc_ref[:, pl.ds(WIDTH, 128)]
    next_ref[...] = (acc_ref[:, pl.ds(0, WIDTH)] + cent_ref[...]) / (mass[:, :1] + 1.0)
    mass_ref[...] = jnp.transpose(mass)[0]
    lse_ref[...] = lse_in[0]


def body(docs, centroids):
    bf16, f32 = jnp.bfloat16, jnp.float32
    dma = pltpu.SemaphoreType.DMA
    flag = pltpu.SemaphoreType.REGULAR
    vmem = pl.BlockSpec(memory_space=pltpu.VMEM)
    acc, lse = pl.pallas_call(
        em_kernel,
        out_shape=(jax.ShapeDtypeStruct((ROWS, WIDE), f32), jax.ShapeDtypeStruct((1, DOCS), f32)),
        in_specs=[pl.BlockSpec(memory_space=pl.ANY)] * 2,
        out_specs=(vmem, vmem),
        scratch_shapes=[
            pltpu.VMEM((DOCS, WIDTH), bf16),
            pltpu.VMEM((WIDTH, DOCS), bf16),
            pltpu.VMEM((ROWS, WIDTH), f32),
            pltpu.VMEM((4, HALF, WIDTH), bf16),
            pltpu.VMEM((4, HALF, WIDTH), bf16),
            pltpu.VMEM((4, 2 * HALF, DOCS), bf16),
            pltpu.VMEM((GROUPS, DOCS), f32),
            pltpu.VMEM((GROUPS, DOCS), f32),
            pltpu.VMEM((8, 1, DOCS), f32),
            pltpu.VMEM((GROUPS, DOCS), f32),
            pltpu.VMEM((4, HALF, WIDE), f32),
            pltpu.VMEM((4, HALF, WIDE), bf16),
            pltpu.VMEM((4, HALF, WIDE), bf16),
            pltpu.VMEM((4, HALF, WIDE), bf16),
            pltpu.VMEM((4, 3, ROWS, WIDE), bf16),
            pltpu.VMEM((3, ROWS, WIDE), bf16),
            pltpu.VMEM((3, ROWS, WIDE), bf16),
            dma, dma, flag, flag,
            dma((4,)), dma((4,)),
            dma((4, 4)), dma((4, 4)),
            dma((4, 4)), dma((4, 4)),
            dma((8,)), dma((8,)),
            dma((4,)), dma((4,)),
            dma((4, 4)), dma((4, 4)),
            dma((4,)), dma((4,)),
        ],
        compiler_params=pltpu.CompilerParams(
            collective_id=0, has_side_effects=True, vmem_limit_bytes=56 * 2**20
        ),
        cost_estimate=pl.CostEstimate(
            flops=4 * DOCS * WIDTH * 1024, bytes_accessed=2 * DOCS * WIDTH, transcendentals=DOCS * 1024
        ),
        name="em_step",
    )(docs, centroids)
    return pl.pallas_call(
        finish_kernel,
        out_shape=(
            jax.ShapeDtypeStruct((ROWS, WIDTH), f32),
            jax.ShapeDtypeStruct((ROWS,), f32),
            jax.ShapeDtypeStruct((DOCS,), f32),
        ),
        in_specs=[vmem] * 3,
        out_specs=(vmem,) * 3,
        name="finish",
    )(acc, lse, centroids)


def solution(mesh):
    in_specs = (P("dev", None), P(("cgrp", "dev"), None))
    out_specs = (P(("cgrp", "dev"), None), P(("cgrp", "dev")), P("dev"))
    return jax.shard_map(body, mesh=mesh, in_specs=in_specs, out_specs=out_specs, check_vma=False)
```

time: 51.3 us -> 46.1 us (0.90)
  Pallas kernels: 50.5 us -> 45.2 us
    pallas_call x1, Pallas kernels: 48.8 us -> 43.5 us  [body(): pl.pallas_call(em_kernel, out_shape=(jax.ShapeDtypeStruct((ROWS, WIDE), f...]
where the time goes in v2:
time: 46.1 us; the launch traced here: 45.9 us
  Pallas kernels  45.2 us (98%)
  between operations  0.64 us (1%)
    pallas_call x1, Pallas kernels, body(): pl.pallas_call(em_kernel, out_shape=(jax.ShapeDtypeStruct((ROWS, WIDE), f...  43.5 us
    pallas_call x1, Pallas kernels, body(): pl.pallas_call(finish_kernel, out_shape=(jax.ShapeDtypeStruct((ROWS, WIDT...  1.74 us

profile of v2, /device:TPU:1, one launch (start us, length us, event | category | flops | bytes accessed | tf_op | source)
XLA Modules:
  0.0 45.9 jit_solution(6431548762119395652)
XLA Ops:
  0.6 43.5 %em_step.1 = (f32[32,1152]{1,0:T(8,128)}, f32[1,2048]{1,0:T(1,128)}) custom-call(bf16[2048,1024]{1,0:T(8,128)(2,1)} %docs_hbm.1, f32[32,1024]{1,0:T(8,128)} %cent_ref.1), custom_call_target="tpu_custom_call" | custom-call | flops 8589934592 | bytes 4194304 | tf_op jit(solution)/shard_map/em_step/pallas_call | solution.py:289
  44.1 1.7 %finish.1 = (f32[32,1024]{1,0:T(8,128)}, f32[32]{0:T(128)}, f32[2048]{0:T(1024)}) custom-call(f32[32,1152]{1,0:T(8,128)} %get-tuple-element.5.acc_ref, f32[1,2048]{1,0:T(1,128)} %get-tuple-element.6.lse_in, f32[32,1024]{1,0:T(8,128)} %cent_ref.1), custom_call_target="tpu_custom_call" | custom-call | tf_op jit(solution)/shard_map/finish/pallas_call | solution.py:329

commit v3 on v2

--- a/solution.py
+++ b/solution.py
@@ -11,6 +11,7 @@
 ROWS = 32
 HALF = 128
 WIDE = WIDTH + 128
+TALL = ROWS * WIDTH // 128 + 16
 SCALE = 0.125
 TILE = 256
 GROUPS = 10
@@ -19,7 +20,7 @@
 def em_kernel(
     docs_hbm, cent_hbm, acc_ref, lse_ref,
     docs, turned, cent, mine, sib, expo, top, total, lses, factor,
-    keep, out_sib, in_sib, out_v, in_v, out_a, in_a,
+    keep, keep_own, out_sib, in_sib, out_v, in_v, out_a, in_a,
     docs_sem, cent_sem, low_sem, high_sem,
     s1, r1, s2, r2, s3, r3, s4, r4, s5, r5, s6, r6, s7, r7,
 ):
@@ -118,17 +119,20 @@
         for da in (1, 3, 2):
             across(da, dj).wait_recv()
 
-    for dv in (1, 3, 2):
-        along_v(dv).start()
-    for da in (1, 3, 2):
-        along_a(da, 0).start()
+    def turn(tiles):
+        for i in tiles:
+            part = pl.ds(i * TILE, TILE)
+            turned[:, part] = jnp.transpose(docs[part, :])
+
+    for k in (1, 3, 2):
+        along_v(k).start()
     across(0, 0).start()
     tell_low()
     tell_high()
+    for k in (1, 3, 2):
+        along_a(k, 0).start()
     load.wait()
-    for i in range(DOCS // TILE):
-        part = pl.ds(i * TILE, TILE)
-        turned[:, part] = jnp.transpose(docs[part, :])
+    turn(range(8))
     for dv in (1, 3, 2):
         along_v(dv).wait_recv()
         for da in (1, 3, 2):
@@ -175,6 +179,14 @@
     pl.semaphore_wait(low_sem, 1)
     for k in (4, 3, 5, 2, 6, 1, 7):
         along_z(k).start()
+    for dv in (1, 2, 3):
+        along_v(dv).wait_send()
+    for da in (1, 2, 3):
+        for dj in range(4):
+            along_a(da, dj).wait_send()
+    for da in range(4):
+        for dj in range(4):
+            across(da, dj).wait_send()
     for k in (1, 7, 2, 6, 3, 5, 4):
         arrived_z(k).wait_recv()
     m = lses[0]
@@ -184,50 +196,90 @@
     lse_ref[...] = lse
     factor[...] = jnp.exp(tops - lse)
 
-    def give(t):
-        return remote(out_sib.at[t], in_sib.at[t], s5.at[t], r5.at[t], sibling)
-
-    def sum_v(t, dv):
+    whole = {t: [(t, 0, WIDE, 0, TALL)] for t in (0, 1, 3)}
+    pieces = {2: [(4, 0, WIDTH // 2, 0, TALL // 2 - 8), (2, WIDTH // 2, WIDE - WIDTH // 2, TALL // 2 - 8, TALL // 2 + 8)]}
+    pieces.update(whole)
+
+    def give(t, piece):
+        sem, col, n, _, _ = piece
+        part = pl.ds(col, n)
+        return remote(out_sib.at[t, :, part], in_sib.at[t, :, part], s5.at[sem], r5.at[sem], sibling)
+
+    def sum_v(t, piece, dv):
+        sem, _, _, first, n = piece
+        part = pl.ds(first, n)
         return remote(
-            out_v.at[t, rows(4 - dv)], in_v.at[t, dv - 1], s6.at[t, dv], r6.at[t, dv], at(0, dv)
+            out_v.at[t, 4 - dv, part], in_v.at[t, dv - 1, part], s6.at[sem, dv], r6.at[sem, dv], at(0, dv)
         )
 
     def sum_a(t):
         return remote(out_a.at[t - 1], in_a.at[t - 1], s7.at[t], r7.at[t], at(-t, 0))
 
-    def weigh(t, other, out):
+    left = lax.broadcasted_iota(jnp.int32, (16, 128), 1) < 64
+
+    def emit(t, col, both):
+        for dj in (2, 3, 1, 0):
+            block = both[dj * ROWS:(dj + 1) * ROWS]
+            out = keep_own if dj == 0 else out_v
+            for j in range(0, both.shape[1], 128):
+                values = block[:, j:j + 128]
+                if col + j == WIDTH:
+                    values = jnp.where(left, values[:16], values[16:])
+                lines = pl.ds((col + j) // 128 * ROWS, values.shape[0])
+                out[t, dj, lines, :] = values.astype(out.dtype)
+
+    def weigh(t, other, save, done):
         parts = [
             expo[t, rows(4 * other + dj)].astype(jnp.float32) * factor[pl.ds(first + step * other, 1), :]
             for dj, (first, step) in enumerate([(0, 2)] * 4 if t == 0 else [(1, 2), (4, 1), (8, 1), (6, 1)])
         ]
         resp = jnp.concatenate(parts, axis=0)
-        mass = jnp.broadcast_to(jnp.sum(resp, axis=1, keepdims=True), (HALF, 128))
-        out[t, :, pl.ds(WIDTH, 128)] = mass.astype(out.dtype)
+        mass = jnp.sum(resp, axis=1, keepdims=True)
         resp = resp.astype(jnp.bfloat16)
-        for j in range(WIDTH // TILE):
-            part = pl.ds(j * TILE, TILE)
-            term = jnp.dot(resp, docs[:, part], preferred_element_type=jnp.float32)
-            out[t, :, part] = term.astype(out.dtype)
+        for piece in pieces[t]:
+            _, col, n, _, _ = piece
+            for j in range(col, col + n, TILE):
+                if j == WIDTH:
+                    save(j, jnp.broadcast_to(mass, (HALF, 128)))
+                else:
+                    save(j, jnp.dot(resp, docs[:, pl.ds(j, TILE)], preferred_element_type=jnp.float32))
+            done(piece)
 
     def theirs(t):
-        weigh(t, 1, out_sib)
-        give(t).start()
+        def save(j, term):
+            out_sib[t, :, pl.ds(j, term.shape[1])] = term.astype(jnp.bfloat16)
+
+        weigh(t, 1, save, lambda piece: give(t, piece).start())
+
+    def send_v(t, piece):
+        for dv in (2, 1, 3):
+            sum_v(t, piece, dv).start()
 
     def ours(t):
-        weigh(t, 0, keep)
-
-    def pair(t):
-        give(t).wait_recv()
-        both = keep[t] + in_sib[t].astype(jnp.float32)
-        keep[t] = both
-        out_v[t] = both.astype(jnp.bfloat16)
-        for dv in (2, 1, 3):
-            sum_v(t, dv).start()
+        for piece in pieces[t]:
+            give(t, piece).wait_recv()
+
+        def save(j, term):
+            emit(t, j, term + in_sib[t, :, pl.ds(j, term.shape[1])].astype(jnp.float32))
+
+        weigh(t, 0, save, lambda piece: send_v(t, piece))
+
+    def ours_first(t):
+        def save(j, term):
+            keep[:, pl.ds(j, term.shape[1])] = term
+
+        weigh(t, 0, save, lambda piece: None)
+        for piece in pieces[t]:
+            _, col, n, _, _ = piece
+            give(t, piece).wait_recv()
+            emit(t, col, keep[:, pl.ds(col, n)] + in_sib[t, :, pl.ds(col, n)].astype(jnp.float32))
+            send_v(t, piece)
 
     def row(t):
-        for dv in (1, 3, 2):
-            sum_v(t, dv).wait_recv()
-        own = keep[t, rows(0)]
+        for piece in pieces[t]:
+            for dv in (1, 3, 2):
+                sum_v(t, piece, dv).wait_recv()
+        own = keep_own[t, 0]
         for dv in (1, 2, 3):
             own = own + in_v[t, dv - 1].astype(jnp.float32)
         if t == 0:
@@ -236,48 +288,44 @@
         sum_a(t).start()
 
     theirs(2)
-    ours(2)
     theirs(1)
-    pair(2)
+    ours_first(2)
+    theirs(3)
     ours(1)
-    theirs(3)
-    pair(1)
+    theirs(0)
     ours(3)
-    theirs(0)
-    pair(3)
     ours(0)
-    pair(0)
+    for k in range(1, 8):
+        along_z(k).wait_send()
+    for t in range(4):
+        for piece in pieces[t]:
+            give(t, piece).wait_send()
     row(2)
     row(1)
     row(3)
+    for t in (2, 1, 3):
+        for dv in (1, 2, 3):
+            for piece in pieces[t]:
+                sum_v(t, piece, dv).wait_send()
     acc = row(0)
     for t in (1, 3, 2):
         sum_a(t).wait_recv()
         acc = acc + in_a[t - 1].astype(jnp.float32)
     acc_ref[...] = acc
 
+    for t in (1, 2, 3):
+        sum_a(t).wait_send()
     for dv in (1, 2, 3):
-        along_v(dv).wait_send()
-    for da in (1, 2, 3):
-        for dj in range(4):
-            along_a(da, dj).wait_send()
-    for da in range(4):
-        for dj in range(4):
-            across(da, dj).wait_send()
-    for k in range(1, 8):
-        along_z(k).wait_send()
-    for t in range(4):
-        give(t).wait_send()
-        for dv in (1, 2, 3):
-            sum_v(t, dv).wait_send()
-        if t:
-            sum_a(t).wait_send()
+        sum_v(0, pieces[0][0], dv).wait_send()
 
 
 def finish_kernel(acc_ref, lse_in, cent_ref, next_ref, mass_ref, lse_ref):
-    mass = acc_ref[:, pl.ds(WIDTH, 128)]
-    next_ref[...] = (acc_ref[:, pl.ds(0, WIDTH)] + cent_ref[...]) / (mass[:, :1] + 1.0)
-    mass_ref[...] = jnp.transpose(mass)[0]
+    packed = acc_ref[pl.ds(WIDTH // 128 * ROWS, 16), :]
+    mass = jnp.concatenate([packed[:, :1], packed[:, 64:65]], axis=0)
+    for j in range(WIDTH // 128):
+        part = pl.ds(j * 128, 128)
+        next_ref[:, part] = (acc_ref[pl.ds(j * ROWS, ROWS), :] + cent_ref[:, part]) / (mass + 1.0)
+    mass_ref[...] = jnp.transpose(jnp.broadcast_to(mass, (ROWS, 128)))[0]
     lse_ref[...] = lse_in[0]
 
 
@@ -288,7 +336,7 @@
     vmem = pl.BlockSpec(memory_space=pltpu.VMEM)
     acc, lse = pl.pallas_call(
         em_kernel,
-        out_shape=(jax.ShapeDtypeStruct((ROWS, WIDE), f32), jax.ShapeDtypeStruct((1, DOCS), f32)),
+        out_shape=(jax.ShapeDtypeStruct((TALL, 128), f32), jax.ShapeDtypeStruct((1, DOCS), f32)),
         in_specs=[pl.BlockSpec(memory_space=pl.ANY)] * 2,
         out_specs=(vmem, vmem),
         scratch_shapes=[
@@ -302,24 +350,25 @@
             pltpu.VMEM((GROUPS, DOCS), f32),
             pltpu.VMEM((8, 1, DOCS), f32),
             pltpu.VMEM((GROUPS, DOCS), f32),
-            pltpu.VMEM((4, HALF, WIDE), f32),
+            pltpu.VMEM((HALF, WIDE), f32),
+            pltpu.VMEM((4, 1, TALL, 128), f32),
             pltpu.VMEM((4, HALF, WIDE), bf16),
             pltpu.VMEM((4, HALF, WIDE), bf16),
-            pltpu.VMEM((4, HALF, WIDE), bf16),
-            pltpu.VMEM((4, 3, ROWS, WIDE), bf16),
-            pltpu.VMEM((3, ROWS, WIDE), bf16),
-            pltpu.VMEM((3, ROWS, WIDE), bf16),
+            pltpu.VMEM((4, 4, TALL, 128), bf16),
+            pltpu.VMEM((4, 3, TALL, 128), bf16),
+            pltpu.VMEM((3, TALL, 128), bf16),
+            pltpu.VMEM((3, TALL, 128), bf16),
             dma, dma, flag, flag,
             dma((4,)), dma((4,)),
             dma((4, 4)), dma((4, 4)),
             dma((4, 4)), dma((4, 4)),
             dma((8,)), dma((8,)),
-            dma((4,)), dma((4,)),
-            dma((4, 4)), dma((4, 4)),
+            dma((5,)), dma((5,)),
+            dma((5, 4)), dma((5, 4)),
             dma((4,)), dma((4,)),
         ],
         compiler_params=pltpu.CompilerParams(
-            collective_id=0, has_side_effects=True, vmem_limit_bytes=56 * 2**20
+            collective_id=0, has_side_effects=True, vmem_limit_bytes=52 * 2**20
         ),
         cost_estimate=pl.CostEstimate(
             flops=4 * DOCS * WIDTH * 1024, bytes_accessed=2 * DOCS * WIDTH, transcendentals=DOCS * 1024
@@ -335,6 +384,7 @@
         ),
         in_specs=[vmem] * 3,
         out_specs=(vmem,) * 3,
+        compiler_params=pltpu.CompilerParams(vmem_limit_bytes=8 * 2**20),
         name="finish",
     )(acc, lse, centroids)
 

time: 46.1 us -> 45.2 us (0.980)
  Pallas kernels: 45.2 us -> 43.5 us
  local copies, waits for them, and re-layouts: 0 us -> 0.9 us
    pallas_call x1, Pallas kernels: 1.74 us -> 0.81 us  [body(): pl.pallas_call(finish_kernel, out_shape=(jax.ShapeDtypeStruct((ROWS, WIDT...]
    unnamed x0 -> x2, local copies, waits for them, and re-layouts: none -> 0.9 us
    pallas_call x1, Pallas kernels: 43.5 us -> 42.7 us  [body(): pl.pallas_call(em_kernel, out_shape=(jax.ShapeDtypeStruct((TALL, 128), f3...]
where the time goes in v3:
time: 45.2 us; the launch traced here: 45 us
  Pallas kernels  43.5 us (96%)
  local copies, waits for them, and re-layouts  0.9 us (2%)
  between operations  0.65 us (1%)
    pallas_call x1, Pallas kernels, body(): pl.pallas_call(em_kernel, out_shape=(jax.ShapeDtypeStruct((TALL, 128), f3...  42.7 us

profile of v3, /device:TPU:1, one launch (start us, length us, event | category | flops | bytes accessed | tf_op | source)
XLA Modules:
  0.0 45.0 jit_solution(4646094442273280531)
XLA Ops:
  0.6 0.0 copy-start
  0.6 0.9 %copy-done = f32[32,1024]{1,0:T(8,128)S(1)} copy-done((f32[32,1024]{1,0:T(8,128)S(1)}, f32[32,1024]{1,0:T(8,128)}, u32[]{:S(2)}) %copy-start) | copy-done | bytes 131096
  1.5 42.7 %em_step.1 = (f32[272,128]{1,0:T(8,128)S(1)}, f32[1,2048]{1,0:T(1,128)S(1)}) custom-call(bf16[2048,1024]{1,0:T(8,128)(2,1)} %docs_hbm.1, f32[32,1024]{1,0:T(8,128)S(1)} %copy-done), custom_call_target="tpu_custom_call" | custom-call | flops 8589934592 | bytes 4194304 | tf_op jit(solution)/shard_map/em_step/pallas_call | solution.py:337
  44.2 0.8 %finish.1 = (f32[32,1024]{1,0:T(8,128)}, f32[32]{0:T(128)}, f32[2048]{0:T(1024)}) custom-call(f32[272,128]{1,0:T(8,128)S(1)} %get-tuple-element.5.acc_ref, f32[1,2048]{1,0:T(1,128)S(1)} %get-tuple-element.6.lse_in, f32[32,1024]{1,0:T(8,128)S(1)} %copy-done), custom_call_target="tpu_custom_call" | custom-call | tf_op jit(solution)/shard_map/finish/pallas_call | solution.py:378
Async XLA Ops:
  0.6 0.9 %copy-start = (f32[32,1024]{1,0:T(8,128)S(1)}, f32[32,1024]{1,0:T(8,128)}, u32[]{:S(2)}) copy-start(f32[32,1024]{1,0:T(8,128)} %cent_ref.1) | copy-start | bytes 393220

commit v4 on v3

--- a/solution.py
+++ b/solution.py
@@ -11,14 +11,15 @@
 ROWS = 32
 HALF = 128
 WIDE = WIDTH + 128
-TALL = ROWS * WIDTH // 128 + 16
+LINES = ROWS * WIDTH // 128
+TALL = LINES + 16
 SCALE = 0.125
 TILE = 256
 GROUPS = 10
 
 
 def em_kernel(
-    docs_hbm, cent_hbm, acc_ref, lse_ref,
+    docs_hbm, cent_hbm, acc_ref, mass_ref, lse_ref,
     docs, turned, cent, mine, sib, expo, top, total, lses, factor,
     keep, keep_own, out_sib, in_sib, out_v, in_v, out_a, in_a,
     docs_sem, cent_sem, low_sem, high_sem,
@@ -196,9 +197,7 @@
     lse_ref[...] = lse
     factor[...] = jnp.exp(tops - lse)
 
-    whole = {t: [(t, 0, WIDE, 0, TALL)] for t in (0, 1, 3)}
-    pieces = {2: [(4, 0, WIDTH // 2, 0, TALL // 2 - 8), (2, WIDTH // 2, WIDE - WIDTH // 2, TALL // 2 - 8, TALL // 2 + 8)]}
-    pieces.update(whole)
+    pieces = {t: [(t, 0, WIDE, 0, TALL)] for t in range(4)}
 
     def give(t, piece):
         sem, col, n, _, _ = piece
@@ -311,7 +310,8 @@
     for t in (1, 3, 2):
         sum_a(t).wait_recv()
         acc = acc + in_a[t - 1].astype(jnp.float32)
-    acc_ref[...] = acc
+    acc_ref[...] = acc[:LINES].astype(jnp.bfloat16)
+    mass_ref[...] = acc[LINES:]
 
     for t in (1, 2, 3):
         sum_a(t).wait_send()
@@ -319,12 +319,12 @@
         sum_v(0, pieces[0][0], dv).wait_send()
 
 
-def finish_kernel(acc_ref, lse_in, cent_ref, next_ref, mass_ref, lse_ref):
-    packed = acc_ref[pl.ds(WIDTH // 128 * ROWS, 16), :]
+def finish_kernel(acc_ref, packed_ref, lse_in, cent_ref, next_ref, mass_ref, lse_ref):
+    packed = packed_ref[...]
     mass = jnp.concatenate([packed[:, :1], packed[:, 64:65]], axis=0)
     for j in range(WIDTH // 128):
         part = pl.ds(j * 128, 128)
-        next_ref[:, part] = (acc_ref[pl.ds(j * ROWS, ROWS), :] + cent_ref[:, part]) / (mass + 1.0)
+        next_ref[:, part] = (acc_ref[pl.ds(j * ROWS, ROWS), :].astype(jnp.float32) + cent_ref[:, part]) / (mass + 1.0)
     mass_ref[...] = jnp.transpose(jnp.broadcast_to(mass, (ROWS, 128)))[0]
     lse_ref[...] = lse_in[0]
 
@@ -334,11 +334,15 @@
     dma = pltpu.SemaphoreType.DMA
     flag = pltpu.SemaphoreType.REGULAR
     vmem = pl.BlockSpec(memory_space=pltpu.VMEM)
-    acc, lse = pl.pallas_call(
+    acc, packed, lse = pl.pallas_call(
         em_kernel,
-        out_shape=(jax.ShapeDtypeStruct((TALL, 128), f32), jax.ShapeDtypeStruct((1, DOCS), f32)),
+        out_shape=(
+            jax.ShapeDtypeStruct((LINES, 128), bf16),
+            jax.ShapeDtypeStruct((16, 128), f32),
+            jax.ShapeDtypeStruct((1, DOCS), f32),
+        ),
         in_specs=[pl.BlockSpec(memory_space=pl.ANY)] * 2,
-        out_specs=(vmem, vmem),
+        out_specs=(vmem,) * 3,
         scratch_shapes=[
             pltpu.VMEM((DOCS, WIDTH), bf16),
             pltpu.VMEM((WIDTH, DOCS), bf16),
@@ -368,7 +372,7 @@
             dma((4,)), dma((4,)),
         ],
         compiler_params=pltpu.CompilerParams(
-            collective_id=0, has_side_effects=True, vmem_limit_bytes=52 * 2**20
+            collective_id=0, has_side_effects=True, vmem_limit_bytes=55072 * 2**10
         ),
         cost_estimate=pl.CostEstimate(
             flops=4 * DOCS * WIDTH * 1024, bytes_accessed=2 * DOCS * WIDTH, transcendentals=DOCS * 1024
@@ -382,11 +386,11 @@
             jax.ShapeDtypeStruct((ROWS,), f32),
             jax.ShapeDtypeStruct((DOCS,), f32),
         ),
-        in_specs=[vmem] * 3,
+        in_specs=[vmem] * 4,
         out_specs=(vmem,) * 3,
         compiler_params=pltpu.CompilerParams(vmem_limit_bytes=8 * 2**20),
         name="finish",
-    )(acc, lse, centroids)
+    )(acc, packed, lse, centroids)
 
 
 def solution(mesh):

time: 45.2 us -> 44.2 us (0.978)
  local copies, waits for them, and re-layouts: 0.9 us -> 0.01 us
    unnamed x2, local copies, waits for them, and re-layouts: 0.9 us -> 0.01 us
where the time goes in v4:
time: 44.2 us; the launch traced here: 44.1 us
  Pallas kernels  43.4 us (98%)
  between operations  0.65 us (1%)
    pallas_call x1, Pallas kernels, body(): pl.pallas_call(em_kernel, out_shape=(jax.ShapeDtypeStruct((LINES, 128), b...  42.6 us

profile of v4, /device:TPU:1, one launch (start us, length us, event | category | flops | bytes accessed | tf_op | source)
XLA Modules:
  0.0 44.1 jit_solution(6190946438274522352)
XLA Ops:
  0.6 0.0 copy-start
  0.6 42.6 %em_step.1 = (bf16[256,128]{1,0:T(8,128)(2,1)S(1)}, f32[16,128]{1,0:T(8,128)S(1)}, f32[1,2048]{1,0:T(1,128)S(1)}) custom-call(bf16[2048,1024]{1,0:T(8,128)(2,1)} %docs_hbm.1, f32[32,1024]{1,0:T(8,128)} %cent_ref.1), custom_call_target="tpu_custom_call" | custom-call | flops 8589934592 | bytes 4194304 | tf_op jit(solution)/shard_map/em_step/pallas_call | solution.py:337
  43.2 0.0 copy-done
  43.3 0.8 %finish.1 = (f32[32,1024]{1,0:T(8,128)}, f32[32]{0:T(128)}, f32[2048]{0:T(1024)}) custom-call(bf16[256,128]{1,0:T(8,128)(2,1)S(1)} %get-tuple-element.6.acc_ref, f32[16,128]{1,0:T(8,128)S(1)} %get-tuple-element.7.packed_ref, f32[1,2048]{1,0:T(1,128)S(1)} %get-tuple-element.8.lse_in, f32[32,1024]{1,0:T(8,128)S(1)} %copy-done), custom_call_target="tpu_custom_call" | custom-call | tf_op jit(solution)/shard_map/finish/pallas_call | solution.py:382
Async XLA Ops:
  0.6 42.6 %copy-start = (f32[32,1024]{1,0:T(8,128)S(1)}, f32[32,1024]{1,0:T(8,128)}, u32[]{:S(2)}) copy-start(f32[32,1024]{1,0:T(8,128)} %cent_ref.1) | copy-start | bytes 393220

commit v5 on v4

--- a/solution.py
+++ b/solution.py
@@ -15,7 +15,7 @@
 TALL = LINES + 16
 SCALE = 0.125
 TILE = 256
-GROUPS = 10
+GROUPS = 8
 
 
 def em_kernel(
@@ -156,14 +156,12 @@
     scores(4, from_mine(1))
     forward_a(3)
     wait_across(1)
-    scores(5, from_sib(1))
-    scores(6, from_mine(3))
+    scores(5, from_sib(1) + from_mine(3))
     forward_a(2)
     wait_across(3)
-    scores(7, from_sib(3))
-    scores(8, from_mine(2))
+    scores(6, from_sib(3) + from_mine(2))
     wait_across(2)
-    scores(9, from_sib(2))
+    scores(7, from_sib(2))
 
     tops = top[...]
     m = jnp.max(tops, axis=0, keepdims=True)
@@ -230,7 +228,7 @@
     def weigh(t, other, save, done):
         parts = [
             expo[t, rows(4 * other + dj)].astype(jnp.float32) * factor[pl.ds(first + step * other, 1), :]
-            for dj, (first, step) in enumerate([(0, 2)] * 4 if t == 0 else [(1, 2), (4, 1), (8, 1), (6, 1)])
+            for dj, (first, step) in enumerate([(0, 2)] * 4 if t == 0 else [(1, 2), (4, 1), (6, 1), (5, 1)])
         ]
         resp = jnp.concatenate(parts, axis=0)
         mass = jnp.sum(resp, axis=1, keepdims=True)

time: 44.2 us -> 43.5 us (0.984)
  Pallas kernels: 43.4 us -> 42.8 us
    pallas_call x1, Pallas kernels: 42.6 us -> 41.9 us  [body(): pl.pallas_call(em_kernel, out_shape=(jax.ShapeDtypeStruct((LINES, 128), b...]
where the time goes in v5:
time: 43.5 us; the launch traced here: 43.4 us
  Pallas kernels  42.8 us (98%)
  between operations  0.65 us (1%)
    pallas_call x1, Pallas kernels, body(): pl.pallas_call(em_kernel, out_shape=(jax.ShapeDtypeStruct((LINES, 128), b...  41.9 us

profile of v5, /device:TPU:1, one launch (start us, length us, event | category | flops | bytes accessed | tf_op | source)
XLA Modules:
  0.0 43.4 jit_solution(8216476323224268948)
XLA Ops:
  0.6 0.0 copy-start
  0.6 41.9 %em_step.1 = (bf16[256,128]{1,0:T(8,128)(2,1)S(1)}, f32[16,128]{1,0:T(8,128)S(1)}, f32[1,2048]{1,0:T(1,128)S(1)}) custom-call(bf16[2048,1024]{1,0:T(8,128)(2,1)} %docs_hbm.1, f32[32,1024]{1,0:T(8,128)} %cent_ref.1), custom_call_target="tpu_custom_call" | custom-call | flops 8589934592 | bytes 4194304 | tf_op jit(solution)/shard_map/em_step/pallas_call | solution.py:335
  42.6 0.0 copy-done
  42.6 0.8 %finish.1 = (f32[32,1024]{1,0:T(8,128)}, f32[32]{0:T(128)}, f32[2048]{0:T(1024)}) custom-call(bf16[256,128]{1,0:T(8,128)(2,1)S(1)} %get-tuple-element.6.acc_ref, f32[16,128]{1,0:T(8,128)S(1)} %get-tuple-element.7.packed_ref, f32[1,2048]{1,0:T(1,128)S(1)} %get-tuple-element.8.lse_in, f32[32,1024]{1,0:T(8,128)S(1)} %copy-done), custom_call_target="tpu_custom_call" | custom-call | tf_op jit(solution)/shard_map/finish/pallas_call | solution.py:380
Async XLA Ops:
  0.6 42.0 %copy-start = (f32[32,1024]{1,0:T(8,128)S(1)}, f32[32,1024]{1,0:T(8,128)}, u32[]{:S(2)}) copy-start(f32[32,1024]{1,0:T(8,128)} %cent_ref.1) | copy-start | bytes 393220

commit v6 on v5

--- a/solution.py
+++ b/solution.py
@@ -15,7 +15,7 @@
 TALL = LINES + 16
 SCALE = 0.125
 TILE = 256
-GROUPS = 8
+GROUPS = 7
 
 
 def em_kernel(
@@ -151,17 +151,16 @@
     told()
     tell_low()
     wait_across(0)
-    scores(3, from_sib(0))
     forward_a(1)
-    scores(4, from_mine(1))
+    scores(3, from_sib(0) + from_mine(1))
     forward_a(3)
     wait_across(1)
-    scores(5, from_sib(1) + from_mine(3))
+    scores(4, from_sib(1) + from_mine(3))
     forward_a(2)
     wait_across(3)
-    scores(6, from_sib(3) + from_mine(2))
+    scores(5, from_sib(3) + from_mine(2))
     wait_across(2)
-    scores(7, from_sib(2))
+    scores(6, from_sib(2))
 
     tops = top[...]
     m = jnp.max(tops, axis=0, keepdims=True)
@@ -228,7 +227,7 @@
     def weigh(t, other, save, done):
         parts = [
             expo[t, rows(4 * other + dj)].astype(jnp.float32) * factor[pl.ds(first + step * other, 1), :]
-            for dj, (first, step) in enumerate([(0, 2)] * 4 if t == 0 else [(1, 2), (4, 1), (6, 1), (5, 1)])
+            for dj, (first, step) in enumerate([(0, 2)] * 4 if t == 0 else [(1, 2), (3, 1), (5, 1), (4, 1)])
         ]
         resp = jnp.concatenate(parts, axis=0)
         mass = jnp.sum(resp, axis=1, keepdims=True)

time: 43.5 us -> 43.5 us (level)
  no operation moved by 1% of the time
where the time goes in v6:
time: 43.5 us; the launch traced here: 43.4 us
  Pallas kernels  42.8 us (98%)
  between operations  0.65 us (1%)
    pallas_call x1, Pallas kernels, body(): pl.pallas_call(em_kernel, out_shape=(jax.ShapeDtypeStruct((LINES, 128), b...  42 us

profile of v6, /device:TPU:1, one launch (start us, length us, event | category | flops | bytes accessed | tf_op | source)
XLA Modules:
  0.0 43.4 jit_solution(7844563753229341996)
XLA Ops:
  0.6 0.0 copy-start
  0.6 42.0 %em_step.1 = (bf16[256,128]{1,0:T(8,128)(2,1)S(1)}, f32[16,128]{1,0:T(8,128)S(1)}, f32[1,2048]{1,0:T(1,128)S(1)}) custom-call(bf16[2048,1024]{1,0:T(8,128)(2,1)} %docs_hbm.1, f32[32,1024]{1,0:T(8,128)} %cent_ref.1), custom_call_target="tpu_custom_call" | custom-call | flops 8589934592 | bytes 4194304 | tf_op jit(solution)/shard_map/em_step/pallas_call | solution.py:334
  42.6 0.0 copy-done
  42.6 0.8 %finish.1 = (f32[32,1024]{1,0:T(8,128)}, f32[32]{0:T(128)}, f32[2048]{0:T(1024)}) custom-call(bf16[256,128]{1,0:T(8,128)(2,1)S(1)} %get-tuple-element.6.acc_ref, f32[16,128]{1,0:T(8,128)S(1)} %get-tuple-element.7.packed_ref, f32[1,2048]{1,0:T(1,128)S(1)} %get-tuple-element.8.lse_in, f32[32,1024]{1,0:T(8,128)S(1)} %copy-done), custom_call_target="tpu_custom_call" | custom-call | tf_op jit(solution)/shard_map/finish/pallas_call | solution.py:379
Async XLA Ops:
  0.6 42.0 %copy-start = (f32[32,1024]{1,0:T(8,128)S(1)}, f32[32,1024]{1,0:T(8,128)}, u32[]{:S(2)}) copy-start(f32[32,1024]{1,0:T(8,128)} %cent_ref.1) | copy-start | bytes 393220
